TPU v7x, 256 devices: a whole 4x4x8 slice. The times are simulated.
256 devices in a mesh: section: 8 (over x, y_lo), seq: 32 (over y_hi, z, core).
Axes of the slice: x: 4, y: 4 (y_hi: 2, y_lo: 2; y = y_hi * 2 + y_lo), z: 8, core: 2. Of those that a mesh axis runs over, the one named last changes fastest.
Arguments:
- acts: bfloat16 [8, 8, 2048, 1536], P('section', None, 'seq'), may hold values from -6 to 6
- attn_proj: bfloat16 [8, 4, 1536, 1536], P('section', None, 'seq'), may hold values from -0.15625 to 0.15625
- modulation: bfloat16 [8, 8, 3, 1536], P('section'), may hold values from -6 to 6
- q_gain: float32 [8, 1536], P('section'), may hold values from 0.8 to 72, as said below
- text_feat: bfloat16 [8, 256, 4096], P(None, 'seq', 'section'), may hold values from -6 to 6
- text_proj: bfloat16 [4096, 1536], P('section'), may hold values from -0.09375 to 0.09375
- text_len: int32 [8], replicated, may hold values from 64 to 256
- kv_index: int32 [16, 4], replicated, may hold values from 0 to 15, as said below
- kv_count: int32 [16], replicated, may hold values from 1 to 4
Outputs:
- received: bfloat16 [8, 8, 2048, 1536], P('section', None, 'seq')
Inputs may be any that keep to these rules, and one draw needn't show every extreme that they name: `q_gain`: heads differ in scale; the gain is the same within a head up to a factor within 0.8 to 1.2 for each feature. `kv_index`: every row starts with its own tile; the first kv_count entries of a row are distinct; entries past kv_count repeat the row's own tile.
All inputs are finite; a program needn't handle non-finite values.
Results may differ from a plain program's by a relative error of at most 0.0075.
The roundings to bfloat16 on the way count: a program that leaves them out, or rounds other values in their place, can miss the bound.
Values may be sent and summed in bfloat16 or wider, within the bound.
No kernel may reach another device: no remote copies, remote signals or barrier semaphores. Data moves between devices by JAX's collectives and lax.ppermute only.
A program may use at most 128 MiB of HBM per device.

v0:
```python
import math

import jax
import jax.numpy as jnp
from jax import lax
from jax.sharding import PartitionSpec as P

HEADS = 12
HEAD_DIM = 128


def shifted(block, axis, distance):
    devices = range(lax.axis_size(axis))
    route = [((i - distance) % len(devices), i) for i in devices]
    return lax.ppermute(block, axis, route)


def unit_rows(values):
    return values * lax.rsqrt(jnp.mean(values * values, axis=-1, keepdims=True) + 1e-06)


def attend(query, keys, values, text_keys, text_values, text_count, kv_index, kv_count):
    length, head_dim = query.shape
    tiles, slots = kv_index.shape
    tile = length // tiles
    group = math.gcd(tiles, max(1, 512 // tile))
    key_tiles = keys.reshape(tiles, tile, head_dim)
    value_tiles = values.reshape(tiles, tile, head_dim)
    scale = 1.0 / math.sqrt(head_dim)
    text_valid = jnp.arange(text_keys.shape[0], dtype=jnp.int32) < text_count

    def block(start):
        lists = lax.dynamic_slice_in_dim(kv_index, start, group, 0)
        counts = lax.dynamic_slice_in_dim(kv_count, start, group, 0)
        rows = lax.dynamic_slice_in_dim(query, start * tile, group * tile, 0).reshape(
            group, tile, head_dim
        )
        near_keys = key_tiles[lists].reshape(group, slots * tile, head_dim)
        near_values = value_tiles[lists].reshape(group, slots * tile, head_dim)
        video_scores = (
            jnp.einsum("gqe,gke->gqk", rows, near_keys, preferred_element_type=jnp.float32) * scale
        )
        text_scores = (
            jnp.einsum("gqe,ke->gqk", rows, text_keys, preferred_element_type=jnp.float32) * scale
        )
        live = jnp.repeat(
            jnp.arange(slots, dtype=jnp.int32)[None, :] < counts[:, None], tile, axis=1
        )
        video_scores = jnp.where(live[:, None, :], video_scores, -jnp.inf)
        text_scores = jnp.where(text_valid[None, None, :], text_scores, -jnp.inf)
        top = jnp.maximum(jnp.max(video_scores, axis=-1), jnp.max(text_scores, axis=-1))[..., None]
        video_exp = jnp.exp(video_scores - top)
        text_exp = jnp.exp(text_scores - top)
        denom = jnp.sum(video_exp, axis=-1, keepdims=True) + jnp.sum(
            text_exp, axis=-1, keepdims=True
        )
        video_probs = (video_exp / denom).astype(jnp.bfloat16)
        text_probs = (text_exp / denom).astype(jnp.bfloat16)
        mixed = jnp.einsum(
            "gqk,gke->gqe", video_probs, near_values, preferred_element_type=jnp.float32
        )
        mixed = mixed + jnp.einsum(
            "gqk,ke->gqe", text_probs, text_values, preferred_element_type=jnp.float32
        )
        return mixed.astype(jnp.bfloat16)

    starts = jnp.arange(tiles // group, dtype=jnp.int32) * group
    return lax.map(block, starts).reshape(length, head_dim)


def body(acts, attn_proj, modulation, q_gain, text_feat, text_proj, text_len, kv_index, kv_count):
    sequences, tokens_here, width = (acts.shape[1], acts.shape[2], acts.shape[3])
    members = lax.axis_size("seq")
    per_device = sequences * HEADS // members
    partial_value = jnp.einsum(
        "std,de->ste", text_feat, text_proj, preferred_element_type=jnp.float32
    )
    text_sum = lax.psum(partial_value, "section")
    text_emb = unit_rows(text_sum).astype(jnp.bfloat16)
    local_weights = attn_proj[0]
    full_weights = lax.all_gather(local_weights, "seq", axis=1, tiled=True)
    inner_weights = full_weights[:3]
    inputs = acts[0].astype(jnp.float32)
    mean = jnp.mean(inputs, axis=-1, keepdims=True)
    variance = jnp.mean((inputs - mean) ** 2, axis=-1, keepdims=True)
    shift = modulation[0, :, 0][:, None, :].astype(jnp.float32)
    scale = modulation[0, :, 1][:, None, :].astype(jnp.float32)
    gate = modulation[0, :, 2][:, None, :].astype(jnp.float32)
    modulated = ((inputs - mean) * lax.rsqrt(variance + 1e-06) * (1.0 + scale) + shift).astype(
        jnp.bfloat16
    )
    heads_w = inner_weights.reshape(3, width, HEADS, HEAD_DIM)
    projected = jnp.einsum(
        "std,kdhe->kshte", modulated, heads_w, preferred_element_type=jnp.float32
    )
    gain = q_gain[0].reshape(HEADS, HEAD_DIM)[None, :, None, :]
    query = (unit_rows(projected[0]) * gain).astype(jnp.bfloat16)
    keys = unit_rows(projected[1]).astype(jnp.bfloat16)
    values = projected[2].astype(jnp.bfloat16)
    text_in = jnp.einsum(
        "std,kdhe->kshte", text_emb, heads_w[1:], preferred_element_type=jnp.float32
    )
    text_keys = unit_rows(text_in[0]).astype(jnp.bfloat16)
    text_values = text_in[1].astype(jnp.bfloat16)

    def to_slots(tensor):
        return tensor.reshape(members, per_device, tensor.shape[2], HEAD_DIM)

    moved = (
        lax.all_to_all(to_slots(query), "seq", split_axis=0, concat_axis=2, tiled=True),
        lax.all_to_all(to_slots(keys), "seq", split_axis=0, concat_axis=2, tiled=True),
        lax.all_to_all(to_slots(values), "seq", split_axis=0, concat_axis=2, tiled=True),
        lax.all_to_all(to_slots(text_keys), "seq", split_axis=0, concat_axis=2, tiled=True),
        lax.all_to_all(to_slots(text_values), "seq", split_axis=0, concat_axis=2, tiled=True),
    )
    slot_ids = lax.axis_index("seq") * per_device + jnp.arange(per_device, dtype=jnp.int32)
    owner = slot_ids // HEADS
    matches = owner[:, None] == jnp.arange(sequences, dtype=jnp.int32)[None, :]
    slot_lens = jnp.sum(jnp.where(matches, text_len[None, :], 0), axis=1)

    def one_slot(item):
        return attend(item[0], item[1], item[2], item[3], item[4], item[5], kv_index, kv_count)

    attended = lax.map(
        one_slot, (moved[0][0], moved[1][0], moved[2][0], moved[3][0], moved[4][0], slot_lens)
    )
    length = attended.shape[1]
    returned = lax.all_to_all(
        attended.reshape(per_device, members, length // members, HEAD_DIM),
        "seq",
        split_axis=1,
        concat_axis=0,
        tiled=True,
    )
    by_token = (
        returned.reshape(sequences, HEADS, tokens_here, HEAD_DIM)
        .transpose(0, 2, 1, 3)
        .reshape(sequences * tokens_here, width)
    )
    output = jnp.dot(by_token, full_weights[3], preferred_element_type=jnp.float32)
    fresh = (inputs + gate * output.reshape(sequences, tokens_here, width)).astype(jnp.bfloat16)
    return shifted(fresh[None], "section", 1)


def solution(mesh):
    in_specs = (
        P("section", None, "seq", None),
        P("section", None, "seq", None),
        P("section", None, None, None),
        P("section", None),
        P(None, "seq", "section"),
        P("section", None),
        P(),
        P(),
        P(),
    )
    out_specs = P("section", None, "seq", None)
    return jax.shard_map(body, mesh=mesh, in_specs=in_specs, out_specs=out_specs, check_vma=False)
```

profile of v0, /device:TPU:1, one launch (start us, length us, event | category | flops | bytes accessed | tf_op | source)
XLA Modules:
  0.0 608.3 jit_solution(8304811448703668890)
XLA Ops:
  8.8 2.0 fusion.30
  13.6 128.6 %all-reduce.2.cloned.1.call-done = f32[8,8,1536]{2,1,0:T(8,128)} async-done(((f32[8,8,1536]{2,1,0:T(8,128)}), f32[8,8,1536]{2,1,0:T(8,128)}) %all-reduce.2.cloned.1.call-update) | async-done | bytes 393232 | tf_op jit(solution)/shard_map/psum | solution.py:78
  143.3 25.0 %all-gather.3.cloned.1.call-done = bf16[1,4,1536,1536]{3,2,1,0:T(8,128)(2,1)} async-done(((bf16[1,4,48,1536]{3,2,1,0:T(8,128)(2,1)}), bf16[1,4,1536,1536]{3,2,1,0:T(8,128)(2,1)}) %all-gather.3.cloned.1.call-update) | async-done | bytes 18874384 | tf_op jit(solution)/shard_map/all_gather | solution.py:81
  168.3 8.0 %slice.62 = bf16[1,2,1536,1536]{3,2,1,0:T(8,128)(2,1)} slice(bf16[1,4,1536,1536]{3,2,1,0:T(8,128)(2,1)} %all-gather.3.cloned.1.call-done), slice={[0:1], [1:3], [0:1536], [0:1536]} | slice | bytes 18874368 | tf_op jit(solution)/shard_map/slice | solution.py:101
  176.3 12.7 %copy.56 = bf16[1,2,1536,1536]{2,3,1,0:T(8,128)(2,1)} copy(bf16[1,2,1536,1536]{3,2,1,0:T(8,128)(2,1)} %slice.62) | data formatting | bytes 18874368 | tf_op jit(solution)/shard_map/slice | solution.py:101
  189.1 5.6 convolution_bitcast_fusion.1
  198.3 5.8 slice.58
  204.1 18.6 %copy.51 = bf16[1,3,1536,1536]{2,3,1,0:T(8,128)(2,1)} copy(bf16[1,3,1536,1536]{3,2,1,0:T(8,128)(2,1)} %slice.58) | data formatting | bytes 28311552 | tf_op jit(solution)/shard_map/slice | solution.py:82
  223.6 4.7 all-to-all-start.3
  228.3 10.4 %convolution_bitcast_fusion = f32[3,8,12,64,128]{4,3,2,0,1:T(8,128)S(1)} fusion(bf16[3,1536,12,128,1]{1,3,2,0,4:T(8,128)(2,1)} %bitcast.188, bf16[1,8,64,1536]{3,2,1,0:T(8,128)(2,1)S(1)} %copy-done.3, f32[8,1536]{1,0:T(8,128)S(1)} %get-tuple-element.247, f32[8,1536]{1,0:T(8,128)S(1)} %add_bitcast_fusion, f32[8,64]{1,0:T(8,128)S(1)} %add_rsqrt_fusion.4, ...), kind=kOutput, calls=%fused_computation.43 | convolution fusion | flops 7252475904 | bytes 25268224 | tf_op jit(solution)/shard_map/std,kdhe->kshte/dot_general | solution.py:93
  238.7 3.7 copy-done.2
  242.4 3.4 multiply_reduce_fusion
  245.8 9.8 %all-to-all-start.4 = ((bf16[32,3,8,128]{3,2,1,0:T(8,128)(2,1)}), bf16[32,3,8,128]{3,2,1,0:T(8,128)(2,1)S(1)}, u32[]{:S(2)}, u32[]{:S(2)}) async-start(bf16[32,3,8,128]{3,2,1,0:T(8,128)(2,1)} %bitcast.39), calls=%async_computation.4 | async-start | bytes 393216 | tf_op jit(solution)/shard_map/all_to_all | solution.py:114
  255.7 3.3 multiply_convert_fusion.1
  258.9 8.4 %all-to-all-done.4 = bf16[32,3,8,128]{3,2,1,0:T(8,128)(2,1)S(1)} async-done(((bf16[32,3,8,128]{3,2,1,0:T(8,128)(2,1)}), bf16[32,3,8,128]{3,2,1,0:T(8,128)(2,1)S(1)}, u32[]{:S(2)}, u32[]{:S(2)}) %all-to-all-start.4) | async-done | bytes 196640 | tf_op jit(solution)/shard_map/all_to_all | solution.py:114
  267.3 5.5 all-to-all-start
  272.8 3.3 multiply_convert_fusion
  276.1 36.6 %all-to-all-done = bf16[32,3,64,128]{3,2,1,0:T(8,128)(2,1)S(1)} async-done(((bf16[32,3,64,128]{3,2,1,0:T(8,128)(2,1)}), bf16[32,3,64,128]{3,2,1,0:T(8,128)(2,1)S(1)}, u32[]{:S(2)}, u32[]{:S(2)}) %all-to-all-start) | async-done | bytes 1572896 | tf_op jit(solution)/shard_map/all_to_all | solution.py:110
  312.7 5.4 all-to-all-start.1
  318.1 3.5 slice.82
  321.6 36.3 %all-to-all-done.1 = bf16[32,3,64,128]{3,2,1,0:T(8,128)(2,1)S(1)} async-done(((bf16[32,3,64,128]{3,2,1,0:T(8,128)(2,1)}), bf16[32,3,64,128]{3,2,1,0:T(8,128)(2,1)S(1)}, u32[]{:S(2)}, u32[]{:S(2)}) %all-to-all-start.1) | async-done | bytes 1572896 | tf_op jit(solution)/shard_map/all_to_all | solution.py:111
  357.9 5.5 all-to-all-start.2
  368.7 34.7 %all-to-all-done.2 = bf16[32,3,64,128]{3,2,1,0:T(8,128)(2,1)} async-done(((bf16[32,3,64,128]{3,2,1,0:T(8,128)(2,1)}), bf16[32,3,64,128]{3,2,1,0:T(8,128)(2,1)}, u32[]{:S(2)}, u32[]{:S(2)}) %all-to-all-start.2) | async-done | bytes 1572896 | tf_op jit(solution)/shard_map/all_to_all | solution.py:112
  403.4 2.8 copy.55
  406.1 105.5 %while.22 = (s32[]{:T(128)}, bf16[3,2048,128]{2,1,0:T(8,128)(2,1)}, bf16[3,2048,128]{2,1,0:T(8,128)(2,1)}, bf16[3,2048,128]{2,1,0:T(8,128)(2,1)}, bf16[3,2048,12...) while((s32[]{:T(128)}, bf16[3,2048,128]{2,1,0:T(8,128)(2,1)}, ...), condition=%wide.region_15.16_spmd, body=%wide.region_8.15_spmd.sunk | while | flops 204603712 | bytes 13678206 | solution.py:124
  410.0 30.4 %while.23 = (s32[]{:T(128)}, bf16[4,4,128,128]{3,2,1,0:T(8,128)(2,1)S(1)}, s32[4]{0:T(128)S(1)}, s32[16]{0:T(128)S(1)}, bf16[2048,128]{1,0:T(8,128)(2,1)S(1)}, /...) while((s32[]{:T(128)}, ...), condition=%wide.region_14.14_spmd.clone, body=%wide.region_9.13_spmd.clone.sunk | while | flops 204603712 | bytes 9221405 | solution.py:68
  445.2 30.4 %while.23 = (s32[]{:T(128)}, bf16[4,4,128,128]{3,2,1,0:T(8,128)(2,1)S(1)}, s32[4]{0:T(128)S(1)}, s32[16]{0:T(128)S(1)}, bf16[2048,128]{1,0:T(8,128)(2,1)S(1)}, /...) while((s32[]{:T(128)}, ...), condition=%wide.region_14.14_spmd.clone, body=%wide.region_9.13_spmd.clone.sunk | while | flops 204603712 | bytes 9221405 | solution.py:68
  480.3 30.4 %while.23 = (s32[]{:T(128)}, bf16[4,4,128,128]{3,2,1,0:T(8,128)(2,1)S(1)}, s32[4]{0:T(128)S(1)}, s32[16]{0:T(128)S(1)}, bf16[2048,128]{1,0:T(8,128)(2,1)S(1)}, /...) while((s32[]{:T(128)}, ...), condition=%wide.region_14.14_spmd.clone, body=%wide.region_9.13_spmd.clone.sunk | while | flops 204603712 | bytes 9221405 | solution.py:68
  511.6 1.6 copy.61
  513.2 45.6 %all_to_all.90 = bf16[3,32,64,128]{3,2,0,1:T(8,128)(2,1)S(1)} all-to-all(bf16[3,32,64,128]{3,2,0,1:T(8,128)(2,1)S(1)} %copy.61), channel_id=1, replica_groups=mesh['section'=8,'seq'=32] {'seq'}, dimensions={1} | all-to-all | bytes 3145728 | tf_op jit(solution)/shard_map/all_to_all | solution.py:128
  558.8 5.1 fusion.25
  565.3 34.4 %collective-permute-done = bf16[1,8,64,1536]{3,2,1,0:T(8,128)(2,1)S(1)} collective-permute-done((bf16[1,8,64,1536]{3,2,1,0:T(8,128)(2,1)S(1)}, bf16[1,8,64,1536]{3,2,1,0:T(8,128)(2,1)S(1)}, u32[]{:S(2)}, u32[]{:S(2)}) %collective-permute-start) | collective-permute-done | bytes 1572896 | tf_op jit(solution)/shard_map/ppermute | solution.py:15
  (330 shorter events, 91.6 us)
Async XLA Ops:
  7.4 1.4 copy-start
  7.4 4.7 copy-start.3
  7.4 5.6 copy-start.7
  7.4 134.8 %all-reduce.2.cloned.1.call-start = ((), (), s32[]{:S(2)}) async-start(), calls=%async_computation.6 | async-start | bytes 786432 | tf_op jit(solution)/shard_map/psum | solution.py:78
  10.8 157.6 %all-gather.3.cloned.1.call-start = ((), (), s32[]{:S(2)}) async-start(), calls=%async_computation.7 | async-start | bytes 19464192 | tf_op jit(solution)/shard_map/all_gather | solution.py:81
  176.3 12.7 %copy-start.6 = (f32[8,8,1536]{2,1,0:T(8,128)S(1)}, f32[8,8,1536]{2,1,0:T(8,128)}, u32[]{:S(2)}) copy-start(f32[8,8,1536]{2,1,0:T(8,128)} %all-reduce.2.cloned.1.call-done) | copy-start | bytes 1179652
  189.0 6.5 %slice-start = ((s8[18874368]{0:T(1024)(128)(4,1)}), s8[4194304]{0:T(1024)(128)(4,1)S(1)}, s32[]{:S(2)}) async-start(s8[18874368]{0:T(1024)(128)(4,1)} %bitcast.186), calls=%async_computation.8 | async-start | bytes 8388608
  189.0 6.5 %slice-start.1 = ((s8[18874368]{0:T(1024)(128)(4,1)}), s8[4194304]{0:T(1024)(128)(4,1)S(1)}, s32[]{:S(2)}) async-start(s8[18874368]{0:T(1024)(128)(4,1)} %bitcast.186), calls=%async_computation.9 | async-start | bytes 8388608
  189.0 7.5 %slice-start.2 = ((s8[18874368]{0:T(1024)(128)(4,1)}), s8[4194304]{0:T(1024)(128)(4,1)S(1)}, s32[]{:S(2)}) async-start(s8[18874368]{0:T(1024)(128)(4,1)} %bitcast.186), calls=%async_computation.10 | async-start | bytes 8388608
  189.1 8.7 %slice-start.3 = ((s8[18874368]{0:T(1024)(128)(4,1)}), s8[4194304]{0:T(1024)(128)(4,1)S(1)}, s32[]{:S(2)}) async-start(s8[18874368]{0:T(1024)(128)(4,1)} %bitcast.186), calls=%async_computation.11 | async-start | bytes 8388608
  189.1 9.3 %slice-start.4 = ((s8[18874368]{0:T(1024)(128)(4,1)}), s8[2097152]{0:T(1024)(128)(4,1)S(1)}, s32[]{:S(2)}) async-start(s8[18874368]{0:T(1024)(128)(4,1)} %bitcast.186), calls=%async_computation.12 | async-start | bytes 4194304
  223.6 22.2 %all-to-all-start.3 = ((bf16[32,3,8,128]{3,2,1,0:T(8,128)(2,1)}), bf16[32,3,8,128]{3,2,1,0:T(8,128)(2,1)S(1)}, u32[]{:S(2)}, u32[]{:S(2)}) async-start(bf16[32,3,8,128]{3,2,1,0:T(8,128)(2,1)} %multiply_convert_fusion.2), calls=%async_computation.3 | async-start | bytes 393216 | tf_op jit(solution)/shard_map/all_to_all | solution.py:113
  238.7 3.7 copy-start.2
  245.8 21.5 %all-to-all-start.4 = ((bf16[32,3,8,128]{3,2,1,0:T(8,128)(2,1)}), bf16[32,3,8,128]{3,2,1,0:T(8,128)(2,1)S(1)}, u32[]{:S(2)}, u32[]{:S(2)}) async-start(bf16[32,3,8,128]{3,2,1,0:T(8,128)(2,1)} %bitcast.39), calls=%async_computation.4 | async-start | bytes 393216 | tf_op jit(solution)/shard_map/all_to_all | solution.py:114
  267.3 8.8 %copy-start.5 = (bf16[32,3,8,128]{3,2,1,0:T(8,128)(2,1)}, bf16[32,3,8,128]{3,2,1,0:T(8,128)(2,1)S(1)}, u32[]{:S(2)}) copy-start(bf16[32,3,8,128]{3,2,1,0:T(8,128)(2,1)S(1)} %all-to-all-done.4) | copy-start | bytes 589828
  267.3 45.4 %all-to-all-start = ((bf16[32,3,64,128]{3,2,1,0:T(8,128)(2,1)}), bf16[32,3,64,128]{3,2,1,0:T(8,128)(2,1)S(1)}, u32[]{:S(2)}, u32[]{:S(2)}) async-start(bf16[32,3,64,128]{3,2,1,0:T(8,128)(2,1)} %multiply_convert_fusion.1), calls=%async_computation | async-start | bytes 3145728 | tf_op jit(solution)/shard_map/all_to_all | solution.py:110
  312.7 45.2 %all-to-all-start.1 = ((bf16[32,3,64,128]{3,2,1,0:T(8,128)(2,1)}), bf16[32,3,64,128]{3,2,1,0:T(8,128)(2,1)S(1)}, u32[]{:S(2)}, u32[]{:S(2)}) async-start(bf16[32,3,64,128]{3,2,1,0:T(8,128)(2,1)} %multiply_convert_fusion), calls=%async_computation.1 | async-start | bytes 3145728 | tf_op jit(solution)/shard_map/all_to_all | solution.py:111
  318.1 45.3 %copy-start.9 = (s32[16,4]{0,1:T(4,128)S(1)}, s32[16,4]{0,1:T(4,128)}, u32[]{:S(2)}) copy-start(s32[16,4]{0,1:T(4,128)} %param.20) | copy-start | bytes 772
  318.1 45.4 %copy-start.10 = (s32[8]{0:T(128)S(1)}, s32[8]{0:T(128)}, u32[]{:S(2)}) copy-start(s32[8]{0:T(128)} %param.19) | copy-start | bytes 100
  357.9 45.4 %all-to-all-start.2 = ((bf16[32,3,64,128]{3,2,1,0:T(8,128)(2,1)}), bf16[32,3,64,128]{3,2,1,0:T(8,128)(2,1)}, u32[]{:S(2)}, u32[]{:S(2)}) async-start(bf16[32,3,64,128]{3,2,1,0:T(8,128)(2,1)} %bitcast.198), calls=%async_computation.2 | async-start | bytes 3145728 | tf_op jit(solution)/shard_map/all_to_all | solution.py:112
  367.4 38.7 %copy-start.11 = (s32[16]{0:T(128)S(1)}, s32[16]{0:T(128)}, u32[]{:S(2)}) copy-start(s32[16]{0:T(128)} %param.21) | copy-start | bytes 196
  511.6 47.3 %copy-start.4 = (bf16[1,8,64,1536]{3,2,1,0:T(8,128)(2,1)S(1)}, bf16[1,8,64,1536]{3,2,1,0:T(8,128)(2,1)}, u32[]{:S(2)}) copy-start(bf16[1,8,64,1536]{3,2,1,0:T(8,128)(2,1)} %param.13) | copy-start | bytes 4718596
  511.6 47.3 %copy-start.8 = (f32[8,1536]{1,0:T(8,128)S(1)}, f32[8,1536]{1,0:T(8,128)}, u32[]{:S(2)}) copy-start(f32[8,1536]{1,0:T(8,128)} %get-tuple-element.246) | copy-start | bytes 147460
  558.8 42.0 %copy-start.1 = (bf16[512,1536]{1,0:T(8,128)(2,1)S(1)}, bf16[512,1536]{1,0:T(8,128)(2,1)}, u32[]{:S(2)}) copy-start(bf16[512,1536]{1,0:T(8,128)(2,1)} %param.18) | copy-start | bytes 4718596
  564.0 35.8 %collective-permute-start = (bf16[1,8,64,1536]{3,2,1,0:T(8,128)(2,1)S(1)}, bf16[1,8,64,1536]{3,2,1,0:T(8,128)(2,1)S(1)}, u32[]{:S(2)}, u32[]{:S(2)}) collective-permute-start(bf16[1,8,64,1536]{3,2,1,0:T(8,128)(2,1)S(1)} %fusion.25), channel_id=1, source_target_pairs={{224,0},{0,32},{32,64},{64,96},{96,128},{128,160},{160,192},{192,2... | collective-permute-start | bytes 4718600 | tf_op jit(solution)/shard_map/ppermute | solution.py:15
Sparse Core Ops, SparseCore 0:
  10.9 131.2 all-reduce.1
Sparse Core Ops, SparseCore 1:
  14.1 154.2 all-gather.2
where the time goes:
time: 612 us; the launch traced here: 608 us
  waiting for transfers between devices  305 us (50%)
  local copies, waits for them, and re-layouts  108 us (18%)
  blocking collectives  45.6 us (7%)
  matrix products  40.8 us (7%)
  starting transfers between devices  32.2 us (5%)
  loops' own time  31.6 us (5%)
  other arithmetic  30.5 us (5%)
  between operations  15.1 us (2%)
    psum x1, waiting for transfers between devices, body(): text_sum = lax.psum(partial_value, 'section')  129 us
    all_to_all x1, blocking collectives, body(): lax.all_to_all(attended.reshape(per_device, members, length // members, H...  45.6 us
    all_to_all x1, waiting for transfers between devices, body(): lax.all_to_all(to_slots(query), 'seq', split_axis=0, concat_axis=2, tiled...  36.6 us
    all_to_all x1, waiting for transfers between devices, body(): lax.all_to_all(to_slots(keys), 'seq', split_axis=0, concat_axis=2, tiled=...  36.3 us
    all_to_all x1, waiting for transfers between devices, body(): lax.all_to_all(to_slots(values), 'seq', split_axis=0, concat_axis=2, tile...  34.7 us
    ppermute x1, waiting for transfers between devices, shifted(): return lax.ppermute(block, axis, route)  34.4 us
    another operation x3, loops' own time, attend(): return lax.map(block, starts).reshape(length, head_dim)  31.5 us
    all_gather x1, waiting for transfers between devices, body(): full_weights = lax.all_gather(local_weights, 'seq', axis=1, tiled=True)  25 us
  transfers between devices with their start and end apart: 8, of which 7 were waited for; matrix products, arithmetic and copies ran while one was open for 5% of the time, Pallas kernels for 0%

commit v1 on v0

v1 whole, which is shorter than its diff:
```python
import math

import jax
import jax.numpy as jnp
from jax import lax
from jax.experimental import pallas as pl
from jax.experimental.pallas import tpu as pltpu
from jax.sharding import Mesh
from jax.sharding import PartitionSpec as P

HEADS = 12
HEAD_DIM = 128
MEMBERS = 4
PER = HEADS // MEMBERS
COLS = PER * HEAD_DIM
SEQ = ("yh", "z", "core")
NEG = -1e30


def unit_rows(values):
    return values * lax.rsqrt(jnp.mean(values * values, axis=-1, keepdims=True) + 1e-06)


def project_kernel(place, m0, m1, m2, m3, w, gain, q, k, v, ws, xs):
    step = pl.program_id(0)
    rows = w.shape[3]
    width = ws.shape[0]

    @pl.when(step == 0)
    def _():
        for z in range(w.shape[0]):
            for member in range(MEMBERS):
                yh, core = member // 2, member % 2
                start = (yh * 16 + z * 2 + core) * rows
                for kind in range(3):
                    ws[start : start + rows, kind * COLS : (kind + 1) * COLS] = w[z, member, kind]

    for part, block in enumerate((m0, m1, m2, m3)):

        @pl.when(step // 2 == part)
        def _(block=block):
            xs[...] = block[...]

    for kind, out in enumerate((q, k, v)):
        made = jnp.dot(
            xs[...], ws[:, kind * COLS : (kind + 1) * COLS], preferred_element_type=jnp.float32
        )
        for head in range(PER):
            lanes = slice(head * HEAD_DIM, (head + 1) * HEAD_DIM)
            mine = made[:, lanes]
            if kind < 2:
                mine = unit_rows(mine)
            if kind == 0:
                mine = mine * gain[:, lanes]
            out[0, :, 0, :, lanes] = mine.astype(jnp.bfloat16).reshape(4, 64, HEAD_DIM)


def project(place, parts, w, gain):
    def part_map(part):
        return lambda i, place: (jnp.clip(i - 2 * part, 0, 1), 0)

    width = parts[0].shape[1]
    half = parts[0].shape[0] // 2
    out_block = pl.BlockSpec(
        (1, 4, 1, 64, COLS), lambda i, place: (i // 4, i % 2, (i // 2) % 2, 0, 0)
    )
    out = jax.ShapeDtypeStruct((2, 8, 2, 64, COLS), jnp.bfloat16)
    return pl.pallas_call(
        project_kernel,
        out_shape=(out, out, out, jax.ShapeDtypeStruct((width, 3 * COLS), jnp.bfloat16)),
        grid_spec=pltpu.PrefetchScalarGridSpec(
            num_scalar_prefetch=1,
            grid=(8,),
            in_specs=[pl.BlockSpec((half, width), part_map(part)) for part in range(4)]
            + [
                pl.BlockSpec(w.shape, lambda i, place: (0,) * 5),
                pl.BlockSpec(gain.shape, lambda i, place: (0, 0)),
            ],
            out_specs=[out_block] * 3
            + [pl.BlockSpec((width, 3 * COLS), lambda i, place: (0, 0))],
            scratch_shapes=[pltpu.VMEM((half, width), jnp.bfloat16)],
        ),
        compiler_params=pltpu.CompilerParams(vmem_limit_bytes=50 * 2**20),
        cost_estimate=pl.CostEstimate(
            flops=2 * 2048 * 1536 * 1152, bytes_accessed=18 * 2**20, transcendentals=0
        ),
        name="project",
    )(place, *parts, w, gain)


def attend_kernel(place, kv_index, kv_count, text_len, text, ws, q, k, v, out, tk, tv):
    yh, z, core = place[0], place[1], place[2]
    made = jnp.dot(text[...], ws[:, COLS:], preferred_element_type=jnp.float32)
    for head in range(PER):
        lanes = slice(head * HEAD_DIM, (head + 1) * HEAD_DIM)
        tk[:, lanes] = unit_rows(made[:, lanes]).astype(jnp.bfloat16)
        tv[:, lanes] = made[:, COLS + head * HEAD_DIM : COLS + (head + 1) * HEAD_DIM].astype(
            jnp.bfloat16
        )
    scale = 1.0 / math.sqrt(HEAD_DIM)
    tile = q.shape[1]
    txt = text.shape[0]
    valid = lax.broadcasted_iota(jnp.int32, (tile, txt), 1) < text_len[z]
    contract = (((1,), (1,)), ((), ()))

    def one_tile(i, carry):
        slot = lax.rem(i + 8 * yh, 16)
        count = kv_count[i]
        near = [lax.rem(kv_index[i, c] + 8 * yh, 16) for c in range(4)]
        for n in range(1, 5):

            @pl.when(count == n)
            def _(n=n):
                for head in range(PER):
                    lanes = slice(head * HEAD_DIM, (head + 1) * HEAD_DIM)
                    rows = q[slot, :, lanes]
                    scores = [
                        lax.dot_general(
                            rows, k[near[c], :, lanes], contract, preferred_element_type=jnp.float32
                        )
                        * scale
                        for c in range(n)
                    ]
                    text_scores = (
                        lax.dot_general(
                            rows, tk[:, lanes], contract, preferred_element_type=jnp.float32
                        )
                        * scale
                    )
                    scores.append(jnp.where(valid, text_scores, NEG))
                    top = jnp.max(scores[-1], axis=-1, keepdims=True)
                    for one in scores[:-1]:
                        top = jnp.maximum(top, jnp.max(one, axis=-1, keepdims=True))
                    exps = [jnp.exp(one - top) for one in scores]
                    denom = jnp.sum(exps[-1], axis=-1, keepdims=True)
                    for one in exps[:-1]:
                        denom = denom + jnp.sum(one, axis=-1, keepdims=True)
                    inverse = 1.0 / denom
                    probs = [(one * inverse).astype(jnp.bfloat16) for one in exps]
                    mixed = jnp.dot(probs[-1], tv[:, lanes], preferred_element_type=jnp.float32)
                    for c in range(n):
                        mixed = mixed + jnp.dot(
                            probs[c], v[near[c], :, lanes], preferred_element_type=jnp.float32
                        )
                    mixed = mixed.astype(jnp.bfloat16)
                    out[2 * i + core, :, lanes] = mixed[: tile // 2]
                    out[2 * i + 1 - core, :, lanes] = mixed[tile // 2 :]

        return carry

    lax.fori_loop(0, 16, one_tile, 0)


def attend(place, kv_index, kv_count, text_len, text, ws, q, k, v):
    smem = pl.BlockSpec(memory_space=pltpu.SMEM)
    vmem = pl.BlockSpec(memory_space=pltpu.VMEM)
    return pl.pallas_call(
        attend_kernel,
        out_shape=jax.ShapeDtypeStruct((32, 64, COLS), jnp.bfloat16),
        in_specs=[smem] * 4 + [vmem] * 5,
        out_specs=vmem,
        scratch_shapes=[
            pltpu.VMEM((text.shape[0], COLS), jnp.bfloat16),
            pltpu.VMEM((text.shape[0], COLS), jnp.bfloat16),
        ],
        compiler_params=pltpu.CompilerParams(vmem_limit_bytes=40 * 2**20),
        cost_estimate=pl.CostEstimate(
            flops=3 * 10**9, bytes_accessed=11 * 2**20, transcendentals=5 * 10**6
        ),
        name="attend",
    )(place, kv_index, kv_count, text_len, text, ws, q, k, v)


def finish_kernel(att, wo, acts, gate, out, xs):
    for one in range(2):
        for member in range(MEMBERS):
            xs[one * 64 : (one + 1) * 64, member * COLS : (member + 1) * COLS] = att[
                member // 2, one, member % 2
            ]
    made = jnp.dot(xs[...], wo[...], preferred_element_type=jnp.float32)
    for one in range(2):
        out[one] = (
            acts[one].astype(jnp.float32)
            + gate[one].astype(jnp.float32) * made[one * 64 : (one + 1) * 64]
        ).astype(jnp.bfloat16)


def finish(att, wo, acts, gate):
    width = acts.shape[2]
    rows = pl.BlockSpec((2, 64, width), lambda i: (i, 0, 0))
    return pl.pallas_call(
        finish_kernel,
        grid=(4,),
        out_shape=jax.ShapeDtypeStruct(acts.shape, jnp.bfloat16),
        in_specs=[
            pl.BlockSpec((2, 2, 2, 64, COLS), lambda i: (0, i, 0, 0, 0)),
            pl.BlockSpec(wo.shape, lambda i: (0, 0)),
            rows,
            pl.BlockSpec((2, 1, width), lambda i: (i, 0, 0)),
        ],
        out_specs=rows,
        scratch_shapes=[pltpu.VMEM((128, width), jnp.bfloat16)],
        compiler_params=pltpu.CompilerParams(vmem_limit_bytes=40 * 2**20),
        cost_estimate=pl.CostEstimate(
            flops=2 * 512 * 1536 * 1536, bytes_accessed=10 * 2**20, transcendentals=0
        ),
        name="finish",
    )(att, wo, acts, gate)


def swap(block, axis):
    return lax.ppermute(block, axis, [(0, 1), (1, 0)])


def body(acts, attn_proj, modulation, q_gain, text_feat, text_proj, text_len, kv_index, kv_count):
    acts, weights, modulation = acts[0], attn_proj[0], modulation[0]
    width = acts.shape[2]
    yh, z, core = (lax.axis_index(name) for name in SEQ)
    member = 2 * yh + core
    place = jnp.stack([yh, z, core]).astype(jnp.int32)

    inputs = acts.astype(jnp.float32)
    mean = jnp.mean(inputs, axis=-1, keepdims=True)
    variance = jnp.mean((inputs - mean) ** 2, axis=-1, keepdims=True)
    shift = modulation[:, 0][:, None, :].astype(jnp.float32)
    scale = modulation[:, 1][:, None, :].astype(jnp.float32)
    modulated = ((inputs - mean) * lax.rsqrt(variance + 1e-06) * (1.0 + scale) + shift).astype(
        jnp.bfloat16
    )
    own = lax.all_to_all(modulated, "z", split_axis=0, concat_axis=0, tiled=True)

    inner = weights[:3].reshape(3, weights.shape[1], MEMBERS, COLS).transpose(2, 0, 1, 3)
    inner = lax.all_to_all(inner, ("yh", "core"), split_axis=0, concat_axis=0, tiled=True)
    inner = lax.all_gather(inner, "z", axis=0)

    part = jnp.dot(
        text_feat.reshape(-1, text_feat.shape[2]), text_proj, preferred_element_type=jnp.float32
    ).reshape(text_feat.shape[0], text_feat.shape[1], width)
    part = lax.all_to_all(part, "section", split_axis=0, concat_axis=0, tiled=True)
    text = unit_rows(jnp.sum(part, axis=0)).astype(jnp.bfloat16)
    text = lax.all_gather(text, SEQ, axis=0, tiled=True)
    route = []
    for s in range(8):
        for y in range(2):
            for zz in range(8):
                for c in range(2):
                    route.append((((s * 2 + y) * 8 + zz) * 2 + c, ((zz * 2 + y) * 8 + s) * 2 + c))
    text = lax.ppermute(text, ("section",) + SEQ, route)

    own = own.reshape(-1, width)
    across = swap(own, "yh")
    near = swap(own, "core")
    far = swap(across, "core")
    gain = lax.dynamic_slice_in_dim(q_gain, member * COLS, COLS, 1)
    q, k, v, ws = project(place, (own, near, across, far), inner, gain)

    outer, inner = lax.optimization_barrier((weights[3], inner))
    outer = lax.all_gather(outer, SEQ, axis=0, tiled=True)

    tiles = (16, 128, COLS)
    attended = attend(
        place,
        kv_index,
        kv_count,
        text_len,
        text,
        ws,
        q.reshape(tiles),
        k.reshape(tiles),
        v.reshape(tiles),
    )
    attended = lax.all_to_all(attended, SEQ, split_axis=0, concat_axis=0, tiled=True)
    gate = modulation[:, 2][:, None, :]
    fresh = finish(attended.reshape(2, 8, 2, 64, COLS), outer, acts, gate)
    return lax.ppermute(fresh[None], "section", [(i, (i + 1) % 8) for i in range(8)])


def solution(mesh):
    fine = Mesh(mesh.devices.reshape(8, 2, 8, 2), ("section",) + SEQ)
    in_specs = (
        P("section", None, SEQ, None),
        P("section", None, SEQ, None),
        P("section", None, None, None),
        P("section", None),
        P(None, SEQ, "section"),
        P("section", None),
        P(),
        P(),
        P(),
    )
    out_specs = P("section", None, SEQ, None)
    return jax.shard_map(body, mesh=fine, in_specs=in_specs, out_specs=out_specs, check_vma=False)
```

time: 612 us -> 404 us (0.66)
  waiting for transfers between devices: 305 us -> 141 us
  blocking collectives: 45.6 us -> 162 us
  local copies, waits for them, and re-layouts: 108 us -> 15.8 us
  Pallas kernels: 0 us -> 47.8 us
  matrix products: 40.8 us -> 1.14 us
  loops' own time: 31.6 us -> 0 us
  other arithmetic: 30.5 us -> 4.26 us
  starting transfers between devices: 32.2 us -> 15.8 us
    psum x1 -> x0, waiting for transfers between devices: 129 us -> none  [body(): text_sum = lax.psum(partial_value, 'section')]
    all_to_all x5 -> x2, waiting for transfers between devices: 116 us -> 0.01 us  [the longest x1 0.01 us: body(): lax.all_to_all(modulated, 'z', split_axis=0, concat_axis=0, tiled=True)]
    all_to_all x1 -> x2, blocking collectives: 45.6 us -> 121 us  [the longest x1 106 us: body(): lax.all_to_all(attended, SEQ, split_axis=0, concat_axis=0, tiled=True)]
    pallas_call x0 -> x3, Pallas kernels: none -> 47.8 us  [the longest x1 25.6 us: attend(): pl.pallas_call(attend_kernel, out_shape=jax.ShapeDtypeStruct((32, 64, COL...]
    slice x6 -> x1, local copies, waits for them, and re-layouts: 49.3 us -> 1.92 us  [body(): weights[:3].reshape(3, weights.shape[1], MEMBERS, COLS)]
    all_gather x1 -> x2, waiting for transfers between devices: 25 us -> 69.9 us  [the longest x1 69.9 us: body(): inner = lax.all_gather(inner, 'z', axis=0)]
    all_gather x0 -> x1, blocking collectives: none -> 41.1 us  [body(): text = lax.all_gather(text, SEQ, axis=0, tiled=True)]
    dot_general x52 -> x1, matrix products: 40.8 us -> 1.14 us  [body(): jnp.dot(text_feat.reshape(-1, text_feat.shape[2]), text_proj, preferred_e...]
  transfers between devices with their start and end apart: 8 -> 9, of which waited for: 7 -> 3; matrix products, arithmetic and copies ran while one was open for 5% -> 2% of each run, Pallas kernels for 0% -> 11%
where the time goes in v1:
time: 404 us; the launch traced here: 402 us
  blocking collectives  162 us (40%)
  waiting for transfers between devices  141 us (35%)
  Pallas kernels  47.8 us (12%)
  local copies, waits for them, and re-layouts  15.8 us (4%)
  starting transfers between devices  15.8 us (4%)
  between operations  13.6 us (3%)
  other arithmetic  4.26 us (1%)
    all_to_all x1, blocking collectives, body(): lax.all_to_all(attended, SEQ, split_axis=0, concat_axis=0, tiled=True)  106 us
    all_gather x1, waiting for transfers between devices, body(): inner = lax.all_gather(inner, 'z', axis=0)  69.9 us
    all_gather x1, blocking collectives, body(): text = lax.all_gather(text, SEQ, axis=0, tiled=True)  41.1 us
    ppermute x3, waiting for transfers between devices, swap(): return lax.ppermute(block, axis, [(0, 1), (1, 0)])  35.8 us
    ppermute x1, waiting for transfers between devices, body(): lax.ppermute(fresh[None], 'section', [(i, (i + 1) % 8) for i in range(8)])  35.7 us
    pallas_call x1, Pallas kernels, attend(): pl.pallas_call(attend_kernel, out_shape=jax.ShapeDtypeStruct((32, 64, COL...  25.6 us
    pallas_call x1, Pallas kernels, project(): pl.pallas_call(project_kernel, out_shape=(out, out, out, jax.ShapeDtypeSt...  18.8 us
    all_to_all x1, blocking collectives, body(): lax.all_to_all(inner, ('yh', 'core'), split_axis=0, concat_axis=0, tiled=...  15.1 us
  transfers between devices with their start and end apart: 9, of which 3 were waited for; matrix products, arithmetic and copies ran while one was open for 2% of the time, Pallas kernels for 11%

profile of v1, /device:TPU:1, one launch (start us, length us, event | category | flops | bytes accessed | tf_op | source)
XLA Modules:
  0.0 401.8 jit_solution(12011537956252213656)
XLA Ops:
  6.5 1.9 slice.19
  8.5 2.0 reshape.47
  10.5 1.1 copy.19
  11.5 15.1 %all_to_all.20 = bf16[4,3,48,384]{3,2,1,0:T(8,128)(2,1)} all-to-all(bf16[4,3,48,384]{3,2,1,0:T(8,128)(2,1)S(1)} %copy.19), channel_id=1, replica_groups=mesh['section'=8,'yh'=2,'z'=8,'core'=2] {'yh','core'}, dimensions={0} | all-to-all | bytes 884736 | tf_op jit(solution)/shard_map/all_to_all | solution.py:233
  26.8 0.3 convert_reduce_fusion
  27.1 0.5 fusion.2
  27.8 2.0 fusion.5
  29.8 7.9 %all-to-all-start.1 = ((bf16[8,64,1536]{2,1,0:T(8,128)(2,1)}), bf16[8,64,1536]{2,1,0:T(8,128)(2,1)}, u32[]{:S(2)}, u32[]{:S(2)}) async-start(bf16[8,64,1536]{2,1,0:T(8,128)(2,1)} %fusion.5), calls=%async_computation.1 | async-start | bytes 3145728 | tf_op jit(solution)/shard_map/all_to_all | solution.py:230
  37.7 1.6 slice_bitcast_fusion
  39.3 69.9 %all-gather.6.cloned.1.call-done = bf16[32,3,48,384]{3,2,1,0:T(8,128)(2,1)} async-done(((bf16[4,3,48,384]{3,2,1,0:T(8,128)(2,1)}), bf16[32,3,48,384]{3,2,1,0:T(8,128)(2,1)}) %all-gather.6.cloned.1.call-update) | async-done | bytes 3538960 | tf_op jit(solution)/shard_map/all_gather | solution.py:234
  109.3 0.1 collective-permute-start.2
  109.4 1.1 fusion.6
  110.5 4.2 %all-to-all-start = ((f32[8,8,1536]{2,1,0:T(8,128)}), f32[8,8,1536]{2,1,0:T(8,128)}, u32[]{:S(2)}, u32[]{:S(2)}) async-start(f32[8,8,1536]{2,1,0:T(8,128)} %fusion.6), calls=%async_computation | async-start | bytes 786432 | tf_op jit(solution)/shard_map/all_to_all | solution.py:239
  114.7 1.0 collective-permute-start.1
  115.6 35.8 %collective-permute-done.2.m2 = bf16[512,1536]{1,0:T(8,128)(2,1)} collective-permute-done((bf16[512,1536]{1,0:T(8,128)(2,1)}, bf16[512,1536]{1,0:T(8,128)(2,1)}, u32[]{:S(2)}, u32[]{:S(2)}) %collective-permute-start.2) | collective-permute-done | bytes 1572896 | tf_op jit(solution)/shard_map/ppermute | solution.py:212
  151.4 1.8 collective-permute-start.3
  153.2 0.1 copy.20.kv_index
  153.3 0.7 constant_dynamic-slice_fusion.gain
  154.0 1.0 reduce_sum.36
  155.0 0.1 multiply_reduce_fusion
  155.2 41.1 %all_gather.12 = bf16[256,1536]{1,0:T(8,128)(2,1)S(1)} all-gather(bf16[8,1536]{1,0:T(8,128)(2,1)S(1)} %multiply_convert_fusion), channel_id=1, replica_groups=mesh['section'=8,'yh'=2,'z'=8,'core'=2] {'yh','z','core'}, dimensions={0}, use_global_device_ids=true | all-gather | bytes 811008 | tf_op jit(solution)/shard_map/all_gather | solution.py:241
  196.4 0.7 collective-permute-start
  197.2 18.8 %project.1 = (bf16[2,8,2,64,384]{4,3,2,1,0:T(8,128)(2,1)S(1)}, bf16[2,8,2,64,384]{4,3,2,1,0:T(8,128)(2,1)S(1)}, bf16[2,8,2,64,384]{4,3,2,1,0:T(8,128)(2,1)}, bf16[1536,1152]{1,0:T(8,128)(2,1)}) custom-call(s32[3]{0:T(128)S(1)} %pad_add_fusion.place, bf16[512,1536]{1,0:T(8,128)(2,1)} %bitcast.6.m0, bf16[512,1536]{1,0:T(8,128)(2,1)} %collective-permute-done.1.m1, ...), custom_call_target="tpu_custom_call" | custom-call | flops 7247757312 | bytes 18874368 | tf_op jit(solution)/shard_map/project/pallas_call | solution.py:68
  216.1 1.4 copy-done.6
  217.5 2.0 copy-done.7
  219.5 25.6 %attend.1 = bf16[32,64,384]{2,1,0:T(8,128)(2,1)S(1)} custom-call(s32[3]{0:T(128)S(1)} %pad_add_fusion.place, s32[16,4]{1,0:T(8,128)S(1)} %copy.20.kv_index, s32[16]{0:T(128)S(1)} %copy-done.4, s32[8]{0:T(128)S(1)} %copy-done.5, bf16[256,1536]{1,0:T(8,128)(2,1)S(1)} %collective-permute-done.text, bf16[1536,1152]{1,0:T(8,128)(2,1)S(1)} %copy-done.7, ...), custom_call_target="tpu_custom_call" | custom-call | flops 3000000000 | bytes 11534336 | tf_op jit(solution)/shard_map/attend/pallas_call | solution.py:157
  245.0 105.9 %all_to_all.21 = bf16[32,64,384]{2,1,0:T(8,128)(2,1)} all-to-all(bf16[32,64,384]{2,1,0:T(8,128)(2,1)S(1)} %attend.1), channel_id=1, replica_groups=mesh['section'=8,'yh'=2,'z'=8,'core'=2] {'yh','z','core'}, dimensions={0} | all-to-all | bytes 3145728 | tf_op jit(solution)/shard_map/all_to_all | solution.py:272
  350.9 1.4 copy-done.2
  352.4 2.3 copy-done.3
  354.7 3.4 finish.1
  358.2 35.7 %collective-permute-done.4 = bf16[1,8,64,1536]{3,2,1,0:T(8,128)(2,1)S(1)} collective-permute-done((bf16[1,8,64,1536]{3,2,1,0:T(8,128)(2,1)S(1)}, bf16[1,8,64,1536]{3,2,1,0:T(8,128)(2,1)S(1)}, u32[]{:S(2)}, u32[]{:S(2)}) %collective-permute-start.4) | collective-permute-done | bytes 1572896 | tf_op jit(solution)/shard_map/ppermute | solution.py:275
  393.9 1.1 copy.28
  (38 shorter events, 0.6 us)
Async XLA Ops:
  6.5 102.8 %copy-start = (bf16[512,1536]{1,0:T(8,128)(2,1)S(1)}, bf16[512,1536]{1,0:T(8,128)(2,1)}, u32[]{:S(2)}) copy-start(bf16[512,1536]{1,0:T(8,128)(2,1)} %param.14) | copy-start | bytes 4718596
  6.5 102.7 %all-gather.6.cloned.1.call-start = ((), (), s32[]{:S(2)}) async-start(), calls=%async_computation.5 | async-start | bytes 3981312 | tf_op jit(solution)/shard_map/all_gather | solution.py:234
  8.5 18.3 %copy-start.8 = (bf16[1,8,3,1536]{3,1,2,0:T(8,128)(2,1)S(1)}, bf16[1,8,3,1536]{3,1,2,0:T(8,128)(2,1)}, u32[]{:S(2)}) copy-start(bf16[1,8,3,1536]{3,1,2,0:T(8,128)(2,1)} %param.11) | copy-start | bytes 221188
  8.5 18.3 %copy-start.1 = (bf16[1,8,64,1536]{3,2,1,0:T(8,128)(2,1)S(1)}, bf16[1,8,64,1536]{3,2,1,0:T(8,128)(2,1)}, u32[]{:S(2)}) copy-start(bf16[1,8,64,1536]{3,2,1,0:T(8,128)(2,1)} %param.9) | copy-start | bytes 4718596
  29.8 79.6 %copy-start.9 = (bf16[8,8,512]{2,1,0:T(8,128)(2,1)S(1)}, bf16[8,8,512]{2,1,0:T(8,128)(2,1)}, u32[]{:S(2)}) copy-start(bf16[8,8,512]{2,1,0:T(8,128)(2,1)} %param.13) | copy-start | bytes 196612
  29.8 79.5 %all-to-all-start.1 = ((bf16[8,64,1536]{2,1,0:T(8,128)(2,1)}), bf16[8,64,1536]{2,1,0:T(8,128)(2,1)}, u32[]{:S(2)}, u32[]{:S(2)}) async-start(bf16[8,64,1536]{2,1,0:T(8,128)(2,1)} %fusion.5), calls=%async_computation.1 | async-start | bytes 3145728 | tf_op jit(solution)/shard_map/all_to_all | solution.py:230
  37.7 313.3 %all-gather.4.cloned.1.call-start = ((), (), s32[]{:S(2)}) async-start(), calls=%async_computation.4 | async-start | bytes 4866048 | tf_op jit(solution)/shard_map/all_gather | solution.py:258
  39.3 113.9 %copy-start.10 = (s32[16,4]{0,1:T(4,128)S(1)}, s32[16,4]{0,1:T(4,128)}, u32[]{:S(2)}) copy-start(s32[16,4]{0,1:T(4,128)} %param.16) | copy-start | bytes 772
  109.3 42.1 %collective-permute-start.2 = (bf16[512,1536]{1,0:T(8,128)(2,1)}, bf16[512,1536]{1,0:T(8,128)(2,1)}, u32[]{:S(2)}, u32[]{:S(2)}) collective-permute-start(bf16[512,1536]{1,0:T(8,128)(2,1)} %bitcast.6.m0), channel_id=1, source_target_pairs={{0,16},{16,0},{1,17},{17,1},{2,18},{18,2},{3,19},{19,3},{4,20},{20... | collective-permute-start | bytes 4718600 | tf_op jit(solution)/shard_map/ppermute | solution.py:212
  110.5 43.5 %all-to-all-start = ((f32[8,8,1536]{2,1,0:T(8,128)}), f32[8,8,1536]{2,1,0:T(8,128)}, u32[]{:S(2)}, u32[]{:S(2)}) async-start(f32[8,8,1536]{2,1,0:T(8,128)} %fusion.6), calls=%async_computation | async-start | bytes 786432 | tf_op jit(solution)/shard_map/all_to_all | solution.py:239
  114.7 82.5 %collective-permute-start.1 = (bf16[512,1536]{1,0:T(8,128)(2,1)}, bf16[512,1536]{1,0:T(8,128)(2,1)}, u32[]{:S(2)}, u32[]{:S(2)}) collective-permute-start(bf16[512,1536]{1,0:T(8,128)(2,1)} %bitcast.6.m0), channel_id=1, source_target_pairs={{0,1},{1,0},{2,3},{3,2},{4,5},{5,4},{6,7},{7,6},{8,9},{9,8},{10,11... | collective-permute-start | bytes 4718600 | tf_op jit(solution)/shard_map/ppermute | solution.py:212
  151.4 45.8 %collective-permute-start.3 = (bf16[512,1536]{1,0:T(8,128)(2,1)}, bf16[512,1536]{1,0:T(8,128)(2,1)}, u32[]{:S(2)}, u32[]{:S(2)}) collective-permute-start(bf16[512,1536]{1,0:T(8,128)(2,1)} %collective-permute-done.2.m2), channel_id=1, source_target_pairs={{0,1},{1,0},{2,3},{3,2},{4,5},{5,4},{6,7},{7,6},{8,9},{9,8},{10,11... | collective-permute-start | bytes 4718600 | tf_op jit(solution)/shard_map/ppermute | solution.py:212
  196.4 19.6 %collective-permute-start = (bf16[256,1536]{1,0:T(8,128)(2,1)S(1)}, bf16[256,1536]{1,0:T(8,128)(2,1)S(1)}, u32[]{:S(2)}, u32[]{:S(2)}) collective-permute-start(bf16[256,1536]{1,0:T(8,128)(2,1)S(1)} %all_gather.12), channel_id=1, source_target_pairs={{0,0},{1,1},{2,32},{3,33},{4,64},{5,65},{6,96},{7,97},{8,128},{9,1... | collective-permute-start | bytes 2359304 | tf_op jit(solution)/shard_map/ppermute | solution.py:248
  197.2 18.8 %copy-start.4 = (s32[16]{0:T(128)S(1)}, s32[16]{0:T(128)}, u32[]{:S(2)}) copy-start(s32[16]{0:T(128)} %kv_count.1) | copy-start | bytes 196
  197.2 18.9 %copy-start.5 = (s32[8]{0:T(128)S(1)}, s32[8]{0:T(128)}, u32[]{:S(2)}) copy-start(s32[8]{0:T(128)} %text_len.1) | copy-start | bytes 100
  216.0 1.4 copy-start.6
  217.5 2.0 copy-start.7
  350.9 1.4 copy-start.2
  352.4 2.3 copy-start.3
  358.1 35.8 %collective-permute-start.4 = (bf16[1,8,64,1536]{3,2,1,0:T(8,128)(2,1)S(1)}, bf16[1,8,64,1536]{3,2,1,0:T(8,128)(2,1)S(1)}, u32[]{:S(2)}, u32[]{:S(2)}) collective-permute-start(bf16[1,8,64,1536]{3,2,1,0:T(8,128)(2,1)S(1)} %bitcast.32), channel_id=1, source_target_pairs={{0,32},{32,64},{64,96},{96,128},{128,160},{160,192},{192,224},{224... | collective-permute-start | bytes 4718600 | tf_op jit(solution)/shard_map/ppermute | solution.py:275
Sparse Core Ops, SparseCore 0:
  26.8 82.3 all-gather.5
  112.0 87.9 all-gather.3
